TPU v7x, 32 devices: a whole 2x2x4 slice. The times are simulated.
32 devices in a mesh: group: 1, node: 8 (over y, x, core), local: 4 (over z).
Axes of the slice: x: 2, y: 2, z: 4, core: 2. Of those that a mesh axis runs over, the one named last changes fastest.
Arguments:
- queries: bfloat16 [256, 64, 128], P(('group', 'node', 'local')), may hold values from -5 to 5
- key_cache: bfloat16 [256, 4, 96, 128], P(('group', 'node', 'local')), may hold values from -5 to 5
- value_cache: bfloat16 [256, 4, 96, 128], P(('group', 'node', 'local')), may hold values from -15 to 15
- fresh_token_keys: bfloat16 [256, 4, 128], P(('group', 'node', 'local')), may hold values from -5 to 5
- new_values: bfloat16 [256, 4, 128], P(('group', 'node', 'local')), may hold values from -15 to 15
- lengths: int32 [256], P(('group', 'node', 'local')), may hold values from 2 to 96, as said below
- hidden_rows: bfloat16 [256, 4096], P(('group', 'node', 'local')), may hold values from -100 to 100
- norm_gain: bfloat16 [4096], replicated, may hold values from 0.099609375 to 1.8984375
- expert_ids: int32 [256, 8], P(('group', 'node', 'local')), may hold values from 0 to 15, all different within a row; in each aligned block of 8 rows (0 to 7, 8 to 15, ...) at most 8 rows name the same one
- route_scores: float32 [256, 8], P(('group', 'node', 'local')), may hold values from 0.1 to 10
- gate_weight: bfloat16 [32, 4096, 768], P(('node', 'local')), may hold values from -0.09375 to 0.09375
- up_weight: bfloat16 [32, 4096, 768], P(('node', 'local')), may hold values from -0.09375 to 0.09375
- down_weight: bfloat16 [32, 768, 4096], P(('node', 'local')), may hold values from -0.4375 to 0.4375
Outputs:
- context: bfloat16 [256, 8192], P(('group', 'node', 'local'))
- weighted_expert_total: bfloat16 [256, 4096], P(('group', 'node', 'local'))
Inputs may be any that keep to these rules, and one draw needn't show every extreme that they name: `expert_ids`: each row names 8 different experts; among the 8 rows of one device no expert is named more than 8 times, and on some device some expert is named exactly 8 times. `lengths`: some request has all 96 slots filled.
All inputs are finite; a program needn't handle non-finite values.
Results may differ from a plain program's by a relative error of at most 0.0065.
Values may be sent and summed in bfloat16 or wider, within the bound.
A program may use at most 128 MiB of HBM per device.

v0:
```python
import math

import jax
import jax.numpy as jnp
from jax import lax
from jax.sharding import PartitionSpec as P


def attend(queries, key_cache, value_cache, fresh_token_keys, new_values, lengths):
    request_count, head_count, head_width = queries.shape
    kv_heads = key_cache.shape[1]
    slot_count = key_cache.shape[2]
    grouped_queries = queries.reshape(request_count, kv_heads, head_count // kv_heads, head_width)
    inverse_scale = 1.0 / math.sqrt(head_width)
    scores = (
        jnp.einsum(
            "bkgd,bkpd->bkgp", grouped_queries, key_cache, preferred_element_type=jnp.float32
        )
        * inverse_scale
    )
    positions = jnp.arange(slot_count, dtype=jnp.int32)
    in_range = positions[None, :] < lengths[:, None]
    scores = jnp.where(in_range[:, None, None, :], scores, -jnp.inf)
    self_token_score = (
        jnp.einsum(
            "uxea,uxa->uxe", grouped_queries, fresh_token_keys, preferred_element_type=jnp.float32
        )
        * inverse_scale
    )
    highest = jnp.maximum(jnp.max(scores, axis=-1), self_token_score)
    exponent = jnp.exp(scores - highest[..., None])
    own_exponent = jnp.exp(self_token_score - highest)
    denominator = jnp.sum(exponent, axis=-1) + own_exponent
    probs = (exponent / denominator[..., None]).astype(jnp.bfloat16)
    own_prob = (own_exponent / denominator).astype(jnp.bfloat16)
    mixed = jnp.einsum("bkgp,bkpd->bkgd", probs, value_cache, preferred_element_type=jnp.float32)
    mixed = (
        mixed
        + own_prob.astype(jnp.float32)[..., None] * new_values.astype(jnp.float32)[:, :, None, :]
    )
    return mixed.reshape(request_count, head_count * head_width).astype(jnp.bfloat16)


def routed_expert_rows(arrived, gate_piece, up_piece, down_piece):
    flattened_tokens = arrived.reshape(-1, arrived.shape[-1])
    gate_proj = jnp.dot(flattened_tokens, gate_piece, preferred_element_type=jnp.float32)
    up_proj = jnp.dot(flattened_tokens, up_piece, preferred_element_type=jnp.float32)
    activated = (jax.nn.silu(gate_proj) * up_proj).astype(jnp.bfloat16)
    return jnp.dot(activated, down_piece, preferred_element_type=jnp.float32)


def per_device(
    queries,
    key_cache,
    value_cache,
    fresh_token_keys,
    new_values,
    lengths,
    hidden_rows,
    norm_gain,
    expert_ids,
    route_scores,
    gate_weight,
    up_weight,
    down_weight,
):
    context = attend(queries, key_cache, value_cache, fresh_token_keys, new_values, lengths)
    row_count, model_width = hidden_rows.shape
    top_count = expert_ids.shape[1]
    node_count = lax.axis_size("node")
    local_count = lax.axis_size("local")
    devices = node_count * local_count
    experts = devices // 2
    capacity = 2 * min(row_count // 2, max(1, top_count * row_count // experts))
    hidden_f32 = hidden_rows.astype(jnp.float32)
    mean_square = jnp.mean(hidden_f32 * hidden_f32, axis=1, keepdims=True)
    normed = (hidden_f32 * lax.rsqrt(mean_square + 1e-06) * norm_gain.astype(jnp.float32)).astype(
        jnp.bfloat16
    )
    gates = route_scores / jnp.sum(route_scores, axis=1, keepdims=True)
    flat_ids = expert_ids.reshape(-1)
    member = (flat_ids[:, None] == jnp.arange(experts, dtype=jnp.int32)[None, :]).astype(jnp.int32)
    earlier = jnp.cumsum(member, axis=0) - member
    slot_index = jnp.sum(earlier * member, axis=1)
    target_slot = (flat_ids * capacity + slot_index).reshape(row_count, top_count)
    slot_range = jnp.arange(experts * capacity, dtype=jnp.int32)
    matches = target_slot[:, :, None] == slot_range[None, None, :]
    collect = jnp.sum(jnp.where(matches, gates[:, :, None], 0.0), axis=1)
    spread = jnp.any(matches, axis=1).astype(jnp.bfloat16)
    outgoing = lax.dot_general(
        spread, normed, (((0,), (0,)), ((), ())), preferred_element_type=jnp.float32
    ).astype(jnp.bfloat16)
    gate_piece = gate_weight[0]
    up_piece = up_weight[0]
    down_piece = down_weight[0]
    doubled = jnp.repeat(outgoing.reshape(experts, capacity, model_width), 2, axis=0)
    arrived = lax.all_to_all(doubled, ("node", "local"), split_axis=0, concat_axis=0, tiled=True)
    partial_value = routed_expert_rows(arrived, gate_piece, up_piece, down_piece).reshape(
        devices, capacity, model_width
    )
    returned = lax.all_to_all(
        partial_value, ("node", "local"), split_axis=0, concat_axis=0, tiled=True
    )
    combined = jnp.sum(returned.reshape(experts, 2, capacity, model_width), axis=1)
    weighted_expert_total = jnp.dot(
        collect,
        combined.reshape(experts * capacity, model_width),
        precision=lax.Precision.HIGHEST,
        preferred_element_type=jnp.float32,
    ).astype(jnp.bfloat16)
    return (context, weighted_expert_total)


def solution(mesh):
    placed = (
        P(("group", "node", "local"), None, None),
        P(("group", "node", "local"), None, None, None),
        P(("group", "node", "local"), None, None, None),
        P(("group", "node", "local"), None, None),
        P(("group", "node", "local"), None, None),
        P(("group", "node", "local")),
        P(("group", "node", "local"), None),
        P(),
        P(("group", "node", "local"), None),
        P(("group", "node", "local"), None),
        P(("node", "local"), None, None),
        P(("node", "local"), None, None),
        P(("node", "local"), None, None),
    )
    return jax.shard_map(
        per_device,
        mesh=mesh,
        in_specs=placed,
        out_specs=(P(("group", "node", "local"), None), P(("group", "node", "local"), None)),
        check_vma=False,
    )
```

profile of v0, /device:TPU:0, one launch (start us, length us, event | category | flops | bytes accessed | tf_op | source)
XLA Modules:
  0.0 169.7 jit_solution(12951049820695238622)
XLA Ops:
  0.6 0.0 copy-start
  0.6 0.8 eq.28
  1.5 1.0 fusion.28
  2.5 0.7 convert_element_type.48
  3.2 0.1 fusion.37
  3.3 0.1 reduce_window_sum.11
  3.4 0.2 select_reduce_fusion.1
  3.5 0.1 reduce_sum.58
  3.6 0.7 multiply_add_fusion
  4.3 0.1 fusion.36
  4.4 1.5 fusion.6
  5.9 0.2 broadcast_in_dim.44
  6.2 0.0 slice-start.2
  6.2 0.0 slice-start
  6.2 54.6 %all_to_all.10 = bf16[32,8,4096]{2,1,0:T(8,128)(2,1)S(1)} all-to-all(bf16[32,8,4096]{2,1,0:T(8,128)(2,1)S(1)} %bitcast.53), channel_id=1, replica_groups=mesh['group'=1,'node'=8,'local'=4] {'node','local'}, dimensions={0} | all-to-all | bytes 4194304 | tf_op jit(solution)/shard_map/all_to_all | solution.py:97
  60.8 1.8 %fusion.4 = f32[256,768]{1,0:T(8,128)S(1)} fusion(bf16[1,4096,768]{2,1,0:T(8,128)(2,1)S(1)} %copy-done.5, bf16[32,8,4096]{2,1,0:T(8,128)(2,1)S(1)} %all_to_all.10), kind=kOutput, calls=%fused_computation.4 | convolution fusion | flops 1610612736 | bytes 9175040 | tf_op jit(solution)/shard_map/dot_general | solution.py:46
  62.7 1.8 %fusion.20 = bf16[32,8,768]{2,1,0:T(8,128)(2,1)S(1)} fusion(bf16[1,4096,768]{2,1,0:T(8,128)(2,1)S(1)} %bitcast.63, bf16[32,8,4096]{2,1,0:T(8,128)(2,1)S(1)} %all_to_all.10, f32[256,768]{1,0:T(8,128)S(1)} %fusion.4), kind=kOutput, calls=%fused_computation.15 | convolution fusion | flops 1611792384 | bytes 9568256 | tf_op jit(solution)/shard_map/dot_general | solution.py:47
  64.5 3.9 %fusion = f32[32,8,4096]{2,1,0:T(8,128)} fusion(bf16[32,8,768]{2,1,0:T(8,128)(2,1)S(1)} %fusion.20, bf16[1,768,4096]{2,1,0:T(8,128)(2,1)S(1)} %bitcast.55), kind=kOutput, calls=%fused_computation | convolution fusion | flops 1610612736 | bytes 10878976 | tf_op jit(solution)/shard_map/dot_general | solution.py:49
  68.4 0.0 copy-start.1
  68.4 4.6 %all-to-all-start.1 = ((f32[32,8,4096]{2,1,0:T(8,128)}), f32[32,8,4096]{2,1,0:T(8,128)}, u32[]{:S(2)}, u32[]{:S(2)}) async-start(f32[32,8,4096]{2,1,0:T(8,128)} %fusion), calls=%async_computation.1 | async-start | bytes 8388608 | tf_op jit(solution)/shard_map/all_to_all | solution.py:101
  73.1 0.1 iota_compare_fusion.2
  73.1 0.2 fusion.38
  73.3 0.6 fusion.42
  73.9 0.3 fusion.27
  74.3 0.4 fusion.26
  74.7 0.8 copy.21
  75.4 0.1 reduce_sum.59
  75.5 0.1 broadcast_divide_fusion
  75.6 0.1 select_reduce_fusion
  75.7 89.5 %all-to-all-done.1 = f32[32,8,4096]{2,1,0:T(8,128)} async-done(((f32[32,8,4096]{2,1,0:T(8,128)}), f32[32,8,4096]{2,1,0:T(8,128)}, u32[]{:S(2)}, u32[]{:S(2)}) %all-to-all-start.1) | async-done | bytes 4194336 | tf_op jit(solution)/shard_map/all_to_all | solution.py:101
  165.3 2.7 %bitcast_reduce_fusion = f32[16,8,4096]{2,1,0:T(8,128)S(1)} fusion(f32[32,8,4096]{2,1,0:T(8,128)} %all-to-all-done.1), kind=kLoop, calls=%fused_computation.9 | loop fusion | flops 524288 | bytes 6291456 | tf_op jit(solution)/shard_map/reduce_sum | solution.py:104
  167.9 1.7 %convolution_convert_fusion.1 = bf16[8,4096]{1,0:T(8,128)(2,1)} fusion(f32[8,128]{1,0:T(8,128)S(1)} %select_reduce_fusion, f32[16,8,4096]{2,1,0:T(8,128)S(1)} %bitcast_reduce_fusion), kind=kOutput, calls=%fused_computation.8 | convolution fusion | flops 50364416 | bytes 2166784 | tf_op jit(solution)/shard_map/dot_general | solution.py:105
  (26 shorter events, 0.1 us)
Async XLA Ops:
  0.6 73.6 %copy-start = (bf16[8,4,96,128]{3,2,1,0:T(8,128)(2,1)S(1)}, bf16[8,4,96,128]{3,2,1,0:T(8,128)(2,1)}, u32[]{:S(2)}) copy-start(bf16[8,4,96,128]{3,2,1,0:T(8,128)(2,1)} %param.15) | copy-start | bytes 2359300
  4.4 56.4 %copy-start.5 = (bf16[1,4096,768]{2,1,0:T(8,128)(2,1)S(1)}, bf16[1,4096,768]{2,1,0:T(8,128)(2,1)}, u32[]{:S(2)}) copy-start(bf16[1,4096,768]{2,1,0:T(8,128)(2,1)} %param.23) | copy-start | bytes 18874372
  6.2 56.5 %slice-start.2 = ((s8[6291456]{0:T(1024)(128)(4,1)}), s8[4194304]{0:T(1024)(128)(4,1)S(1)}, s32[]{:S(2)}) async-start(s8[6291456]{0:T(1024)(128)(4,1)} %bitcast.62), calls=%async_computation.4 | async-start | bytes 8388608
  6.2 58.3 %slice-start = ((s8[6291456]{0:T(1024)(128)(4,1)}), s8[2097152]{0:T(1024)(128)(4,1)S(1)}, s32[]{:S(2)}) async-start(s8[6291456]{0:T(1024)(128)(4,1)} %bitcast.54), calls=%async_computation.2 | async-start | bytes 4194304
  60.8 1.8 %slice-start.3 = ((s8[6291456]{0:T(1024)(128)(4,1)}), s8[2097152]{0:T(1024)(128)(4,1)S(1)}, s32[]{:S(2)}) async-start(s8[6291456]{0:T(1024)(128)(4,1)} %bitcast.62), calls=%async_computation.5 | async-start | bytes 4194304
  60.8 3.7 %slice-start.1 = ((s8[6291456]{0:T(1024)(128)(4,1)}), s8[4194304]{0:T(1024)(128)(4,1)S(1)}, s32[]{:S(2)}) async-start(s8[6291456]{0:T(1024)(128)(4,1)} %bitcast.54), calls=%async_computation.3 | async-start | bytes 8388608
  68.4 4.6 %copy-start.4 = (bf16[8,4,128]{2,1,0:T(4,128)(2,1)S(1)}, bf16[8,4,128]{2,1,0:T(4,128)(2,1)}, u32[]{:S(2)}) copy-start(bf16[8,4,128]{2,1,0:T(4,128)(2,1)} %param.17) | copy-start | bytes 24580
  68.4 4.7 %copy-start.7 = (s32[8]{0:T(128)S(1)}, s32[8]{0:T(128)}, u32[]{:S(2)}) copy-start(s32[8]{0:T(128)} %param.18) | copy-start | bytes 100
  68.4 4.7 %copy-start.2 = (bf16[8,64,128]{2,1,0:T(8,128)(2,1)S(1)}, bf16[8,64,128]{2,1,0:T(8,128)(2,1)}, u32[]{:S(2)}) copy-start(bf16[8,64,128]{2,1,0:T(8,128)(2,1)} %param.13) | copy-start | bytes 393220
  68.4 4.7 %copy-start.6 = (bf16[8,4,128]{2,1,0:T(4,128)(2,1)S(1)}, bf16[8,4,128]{2,1,0:T(4,128)(2,1)}, u32[]{:S(2)}) copy-start(bf16[8,4,128]{2,1,0:T(4,128)(2,1)} %param.16) | copy-start | bytes 24580
  68.4 4.9 %copy-start.1 = (bf16[8,4,96,128]{3,2,1,0:T(8,128)(2,1)S(1)}, bf16[8,4,96,128]{3,2,1,0:T(8,128)(2,1)}, u32[]{:S(2)}) copy-start(bf16[8,4,96,128]{3,2,1,0:T(8,128)(2,1)} %param.14) | copy-start | bytes 2359300
  68.4 7.0 %copy-start.3 = (f32[8,8]{1,0:T(8,128)S(1)}, f32[8,8]{1,0:T(8,128)}, u32[]{:S(2)}) copy-start(f32[8,8]{1,0:T(8,128)} %param.22) | copy-start | bytes 772
  68.4 96.8 %all-to-all-start.1 = ((f32[32,8,4096]{2,1,0:T(8,128)}), f32[32,8,4096]{2,1,0:T(8,128)}, u32[]{:S(2)}, u32[]{:S(2)}) async-start(f32[32,8,4096]{2,1,0:T(8,128)} %fusion), calls=%async_computation.1 | async-start | bytes 8388608 | tf_op jit(solution)/shard_map/all_to_all | solution.py:101
where the time goes:
time: 171 us; the launch traced here: 170 us
  waiting for transfers between devices  89.5 us (52%)
  blocking collectives  54.6 us (32%)
  matrix products  11.9 us (7%)
  other arithmetic  6.22 us (4%)
  starting transfers between devices  4.59 us (3%)
  local copies, waits for them, and re-layouts  1.97 us (1%)
    all_to_all x1, waiting for transfers between devices, per_device(): lax.all_to_all(partial_value, ('node', 'local'), split_axis=0, concat_axi...  89.5 us
    all_to_all x1, blocking collectives, per_device(): lax.all_to_all(doubled, ('node', 'local'), split_axis=0, concat_axis=0, t...  54.6 us
    all_to_all x1, starting transfers between devices, per_device(): lax.all_to_all(partial_value, ('node', 'local'), split_axis=0, concat_axi...  4.59 us
    dot_general x1, matrix products, routed_expert_rows(): return jnp.dot(activated, down_piece, preferred_element_type=jnp.float32)  3.86 us
  transfers between devices with their start and end apart: 1, of which 1 were waited for; matrix products, arithmetic and copies ran while one was open for 2% of the time, Pallas kernels for 0%

commit v1 on v0

--- a/solution.py
+++ b/solution.py
@@ -66,48 +66,31 @@
 ):
     context = attend(queries, key_cache, value_cache, fresh_token_keys, new_values, lengths)
     row_count, model_width = hidden_rows.shape
-    top_count = expert_ids.shape[1]
-    node_count = lax.axis_size("node")
-    local_count = lax.axis_size("local")
-    devices = node_count * local_count
+    axes = ("node", "local")
+    devices = lax.axis_size("node") * lax.axis_size("local")
     experts = devices // 2
-    capacity = 2 * min(row_count // 2, max(1, top_count * row_count // experts))
     hidden_f32 = hidden_rows.astype(jnp.float32)
     mean_square = jnp.mean(hidden_f32 * hidden_f32, axis=1, keepdims=True)
     normed = (hidden_f32 * lax.rsqrt(mean_square + 1e-06) * norm_gain.astype(jnp.float32)).astype(
         jnp.bfloat16
     )
     gates = route_scores / jnp.sum(route_scores, axis=1, keepdims=True)
-    flat_ids = expert_ids.reshape(-1)
-    member = (flat_ids[:, None] == jnp.arange(experts, dtype=jnp.int32)[None, :]).astype(jnp.int32)
-    earlier = jnp.cumsum(member, axis=0) - member
-    slot_index = jnp.sum(earlier * member, axis=1)
-    target_slot = (flat_ids * capacity + slot_index).reshape(row_count, top_count)
-    slot_range = jnp.arange(experts * capacity, dtype=jnp.int32)
-    matches = target_slot[:, :, None] == slot_range[None, None, :]
-    collect = jnp.sum(jnp.where(matches, gates[:, :, None], 0.0), axis=1)
-    spread = jnp.any(matches, axis=1).astype(jnp.bfloat16)
-    outgoing = lax.dot_general(
-        spread, normed, (((0,), (0,)), ((), ())), preferred_element_type=jnp.float32
-    ).astype(jnp.bfloat16)
-    gate_piece = gate_weight[0]
-    up_piece = up_weight[0]
-    down_piece = down_weight[0]
-    doubled = jnp.repeat(outgoing.reshape(experts, capacity, model_width), 2, axis=0)
-    arrived = lax.all_to_all(doubled, ("node", "local"), split_axis=0, concat_axis=0, tiled=True)
-    partial_value = routed_expert_rows(arrived, gate_piece, up_piece, down_piece).reshape(
-        devices, capacity, model_width
+    matches = expert_ids[:, :, None] == jnp.arange(experts, dtype=jnp.int32)[None, None, :]
+    dense_gates = jnp.sum(jnp.where(matches, gates[:, :, None], 0.0), axis=1)
+    tokens = lax.all_gather(normed, axes, axis=0, tiled=True)
+    all_gates = lax.all_gather(dense_gates, axes, axis=0, tiled=True)
+    mine = (lax.axis_index("node") * lax.axis_size("local") + lax.axis_index("local")) // 2
+    column = jnp.sum(
+        jnp.where(jnp.arange(experts, dtype=jnp.int32)[None, :] == mine, all_gates, 0.0),
+        axis=1,
+        keepdims=True,
     )
+    produced = routed_expert_rows(tokens, gate_weight[0], up_weight[0], down_weight[0])
+    weighted = (produced * column).astype(jnp.bfloat16)
     returned = lax.all_to_all(
-        partial_value, ("node", "local"), split_axis=0, concat_axis=0, tiled=True
+        weighted.reshape(devices, row_count, model_width), axes, split_axis=0, concat_axis=0, tiled=True
     )
-    combined = jnp.sum(returned.reshape(experts, 2, capacity, model_width), axis=1)
-    weighted_expert_total = jnp.dot(
-        collect,
-        combined.reshape(experts * capacity, model_width),
-        precision=lax.Precision.HIGHEST,
-        preferred_element_type=jnp.float32,
-    ).astype(jnp.bfloat16)
+    weighted_expert_total = jnp.sum(returned.astype(jnp.float32), axis=0).astype(jnp.bfloat16)
     return (context, weighted_expert_total)
 
 

time: 171 us -> 160 us (0.936)
  waiting for transfers between devices: 89.5 us -> 44 us
  blocking collectives: 54.6 us -> 71 us
  between operations: 0.86 us -> 14.2 us
  matrix products: 11.9 us -> 19.4 us
    all_gather x0 -> x1, blocking collectives: none -> 71 us  [per_device(): all_gates = lax.all_gather(dense_gates, axes, axis=0, tiled=True)]
    all_to_all x1 -> x0, blocking collectives: 54.6 us -> none  [per_device(): lax.all_to_all(doubled, ('node', 'local'), split_axis=0, concat_axis=0, t...]
    all_to_all x1, waiting for transfers between devices: 89.5 us -> 44 us  [per_device(): lax.all_to_all(weighted.reshape(devices, row_count, model_width), axes, s...]
    dot_general x1, matrix products: 3.86 us -> 10.8 us  [routed_expert_rows(): return jnp.dot(activated, down_piece, preferred_element_type=jnp.float32)]
    dot_general x3 -> x0, matrix products: 5.05 us -> none  [the longest x1 1.84 us: routed_expert_rows(): jnp.dot(flattened_tokens, up_piece, preferred_element_type=jnp.float32)]
    dot_general x1, matrix products: 1.79 us -> 6.26 us  [routed_expert_rows(): jnp.dot(flattened_tokens, gate_piece, preferred_element_type=jnp.float32)]
    all_to_all x1, starting transfers between devices: 4.59 us -> 2.87 us  [per_device(): lax.all_to_all(weighted.reshape(devices, row_count, model_width), axes, s...]
  transfers between devices with their start and end apart: 1 -> 2, of which waited for: 1 -> 1; matrix products, arithmetic and copies ran while one was open for 2% -> 4% of each run, Pallas kernels for 0% -> 0%
where the time goes in v1:
time: 160 us; the launch traced here: 159 us
  blocking collectives  71 us (44%)
  waiting for transfers between devices  44 us (28%)
  matrix products  19.4 us (12%)
  between operations  14.2 us (9%)
  other arithmetic  7.09 us (4%)
  starting transfers between devices  2.91 us (2%)
    all_gather x1, blocking collectives, per_device(): all_gates = lax.all_gather(dense_gates, axes, axis=0, tiled=True)  71 us
    all_to_all x1, waiting for transfers between devices, per_device(): lax.all_to_all(weighted.reshape(devices, row_count, model_width), axes, s...  44 us
    dot_general x1, matrix products, routed_expert_rows(): return jnp.dot(activated, down_piece, preferred_element_type=jnp.float32)  10.8 us
    dot_general x1, matrix products, routed_expert_rows(): jnp.dot(flattened_tokens, gate_piece, preferred_element_type=jnp.float32)  6.26 us
  transfers between devices with their start and end apart: 2, of which 1 were waited for; matrix products, arithmetic and copies ran while one was open for 4% of the time, Pallas kernels for 0%

profile of v1, /device:TPU:0, one launch (start us, length us, event | category | flops | bytes accessed | tf_op | source)
XLA Modules:
  0.0 159.3 jit_solution(6892847063858222353)
XLA Ops:
  7.2 0.0 copy-start
  7.2 0.0 all-gather.2.cloned.1.call-start
  7.2 0.8 convert_element_type.42
  8.0 1.0 fusion.27
  9.0 1.6 fusion.29
  10.5 0.0 all-gather.2.cloned.1.call-update
  10.6 0.8 reduce_sum.59
  11.4 0.8 broadcast_divide_fusion
  12.1 0.8 select_reduce_fusion.1
  12.9 71.0 %all_gather.7 = f32[256,16]{1,0:T(8,128)S(1)} all-gather(f32[8,16]{1,0:T(8,128)S(1)} %select_reduce_fusion.1), channel_id=1, replica_groups=mesh['group'=1,'node'=8,'local'=4] {'node','local'}, dimensions={0}, use_global_device_ids=true | all-gather | bytes 16896 | tf_op jit(solution)/shard_map/all_gather | solution.py:81
  83.9 0.1 select_reduce_fusion
  84.1 0.0 all-gather.2.cloned.1.call-done
  84.1 0.0 copy-start.3
  84.1 6.3 %fusion.4 = f32[256,768]{1,0:T(8,128)} fusion(bf16[256,4096]{1,0:T(8,128)(2,1)} %all-gather.2.cloned.1.call-done, bf16[1,4096,768]{2,1,0:T(8,128)(2,1)} %param.23), kind=kOutput, calls=%fused_computation.4 | convolution fusion | flops 1610612736 | bytes 9175040 | tf_op jit(solution)/shard_map/dot_general | solution.py:46
  90.4 0.0 copy-done.3
  90.4 10.8 %fusion.12 = bf16[32,8,4096]{2,1,0:T(8,128)(2,1)} fusion(bf16[1,768,4096]{2,1,0:T(8,128)(2,1)} %param.25, f32[256]{0:T(256)S(1)} %select_reduce_fusion, bf16[256,4096]{1,0:T(8,128)(2,1)S(1)} %copy-done.3, bf16[1,4096,768]{2,1,0:T(8,128)(2,1)} %param.24, f32[256,768]{1,0:T(8,128)} %fusion.4), kind=kOutput, calls=%fused_computation.8 | convolution fusion | flops 3224502272 | bytes 17564672 | tf_op jit(solution)/shard_map/dot_general | solution.py:49
  101.1 0.0 copy-start.2
  101.1 0.0 copy-start.5
  101.2 2.9 %all-to-all-start = ((bf16[32,8,4096]{2,1,0:T(8,128)(2,1)}), bf16[32,8,4096]{2,1,0:T(8,128)(2,1)S(1)}, u32[]{:S(2)}, u32[]{:S(2)}) async-start(bf16[32,8,4096]{2,1,0:T(8,128)(2,1)} %fusion.12), calls=%async_computation | async-start | bytes 4194304 | tf_op jit(solution)/shard_map/all_to_all | solution.py:90
  104.0 0.0 copy-done.2
  104.1 0.0 copy-done.5
  104.1 0.1 iota_compare_fusion.1
  104.1 0.0 copy-done.1
  104.1 0.0 copy-done.4
  104.2 0.2 fusion.32
  104.3 1.7 %fusion.37 = (f32[8,4,16]{2,1,0:T(4,128)S(1)}, f32[8,4,16,96]{3,2,1,0:T(8,128)S(1)}) fusion(bf16[8,4,16,128]{3,2,1,0:T(8,128)(2,1)S(1)} %bitcast.41, bf16[8,4,96,128]{3,2,1,0:T(8,128)(2,1)} %param.14, pred[8,96]{1,0:T(8,128)(4,1)S(1)} %iota_compare_fusion.1), kind=kOutput, calls=%fused_computation.42 | convolution fusion | flops 12729856 | bytes 1116928 | tf_op jit(solution)/shard_map/bkgd,bkpd->bkgp/dot_general | solution.py:16
  106.1 0.3 fusion.26
  106.4 0.0 copy-done
  106.4 0.4 fusion.22
  106.8 0.8 copy.23
  107.6 44.0 %all-to-all-done = bf16[32,8,4096]{2,1,0:T(8,128)(2,1)S(1)} async-done(((bf16[32,8,4096]{2,1,0:T(8,128)(2,1)}), bf16[32,8,4096]{2,1,0:T(8,128)(2,1)S(1)}, u32[]{:S(2)}, u32[]{:S(2)}) %all-to-all-start) | async-done | bytes 2097184 | tf_op jit(solution)/shard_map/all_to_all | solution.py:90
  151.5 0.9 reduce_sum.62
  (7 shorter events, 0.1 us)
Async XLA Ops:
  7.2 99.3 %copy-start = (bf16[8,4,96,128]{3,2,1,0:T(8,128)(2,1)S(1)}, bf16[8,4,96,128]{3,2,1,0:T(8,128)(2,1)}, u32[]{:S(2)}) copy-start(bf16[8,4,96,128]{3,2,1,0:T(8,128)(2,1)} %param.15) | copy-start | bytes 2359300
  7.2 76.9 %all-gather.2.cloned.1.call-start = ((), (), s32[]{:S(2)}) async-start(), calls=%async_computation.1 | async-start | bytes 2162688 | tf_op jit(solution)/shard_map/all_gather | solution.py:80
  84.1 6.3 %copy-start.3 = (bf16[256,4096]{1,0:T(8,128)(2,1)S(1)}, bf16[256,4096]{1,0:T(8,128)(2,1)}, u32[]{:S(2)}) copy-start(bf16[256,4096]{1,0:T(8,128)(2,1)} %all-gather.2.cloned.1.call-done) | copy-start | bytes 6291460
  101.1 2.9 %copy-start.2 = (bf16[8,4,128]{2,1,0:T(4,128)(2,1)S(1)}, bf16[8,4,128]{2,1,0:T(4,128)(2,1)}, u32[]{:S(2)}) copy-start(bf16[8,4,128]{2,1,0:T(4,128)(2,1)} %param.17) | copy-start | bytes 24580
  101.1 2.9 %copy-start.5 = (s32[8]{0:T(128)S(1)}, s32[8]{0:T(128)}, u32[]{:S(2)}) copy-start(s32[8]{0:T(128)} %param.18) | copy-start | bytes 100
  101.1 3.0 %copy-start.1 = (bf16[8,64,128]{2,1,0:T(8,128)(2,1)S(1)}, bf16[8,64,128]{2,1,0:T(8,128)(2,1)}, u32[]{:S(2)}) copy-start(bf16[8,64,128]{2,1,0:T(8,128)(2,1)} %param.13) | copy-start | bytes 393220
  101.1 3.0 %copy-start.4 = (bf16[8,4,128]{2,1,0:T(4,128)(2,1)S(1)}, bf16[8,4,128]{2,1,0:T(4,128)(2,1)}, u32[]{:S(2)}) copy-start(bf16[8,4,128]{2,1,0:T(4,128)(2,1)} %param.16) | copy-start | bytes 24580
  101.2 50.4 %all-to-all-start = ((bf16[32,8,4096]{2,1,0:T(8,128)(2,1)}), bf16[32,8,4096]{2,1,0:T(8,128)(2,1)S(1)}, u32[]{:S(2)}, u32[]{:S(2)}) async-start(bf16[32,8,4096]{2,1,0:T(8,128)(2,1)} %fusion.12), calls=%async_computation | async-start | bytes 4194304 | tf_op jit(solution)/shard_map/all_to_all | solution.py:90
Sparse Core Ops, SparseCore 0:
  11.5 59.4 all-gather.1

commit v2 on v1

--- a/solution.py
+++ b/solution.py
@@ -1,8 +1,11 @@
+import functools
 import math
 
 import jax
 import jax.numpy as jnp
 from jax import lax
+from jax.experimental import pallas as pl
+from jax.experimental.pallas import tpu as pltpu
 from jax.sharding import PartitionSpec as P
 
 
@@ -41,12 +44,230 @@
     return mixed.reshape(request_count, head_count * head_width).astype(jnp.bfloat16)
 
 
-def routed_expert_rows(arrived, gate_piece, up_piece, down_piece):
-    flattened_tokens = arrived.reshape(-1, arrived.shape[-1])
-    gate_proj = jnp.dot(flattened_tokens, gate_piece, preferred_element_type=jnp.float32)
-    up_proj = jnp.dot(flattened_tokens, up_piece, preferred_element_type=jnp.float32)
-    activated = (jax.nn.silu(gate_proj) * up_proj).astype(jnp.bfloat16)
-    return jnp.dot(activated, down_piece, preferred_element_type=jnp.float32)
+def exchange_orders(node_count, local_count):
+    local_bits = [("local", 1 << b) for b in reversed(range(local_count.bit_length() - 1))]
+    node_bits = [("node", 1 << b) for b in reversed(range(1, node_count.bit_length() - 1))]
+    core = [("node", 1)]
+    weights = {bit: 1 << k for k, bit in enumerate(local_bits + node_bits + core)}
+    return weights, (local_bits + node_bits + core, local_bits + node_bits[::-1] + core)
+
+
+def runs_of(slots):
+    runs = []
+    for slot in sorted(slots):
+        if runs and runs[-1][0] + runs[-1][1] == slot:
+            runs[-1][1] += 1
+        else:
+            runs.append([slot, 1])
+    return runs
+
+
+def gather_plan(weights, order):
+    held, stages = [0], []
+    for bit in order:
+        stages.append((bit, runs_of(held)))
+        held = held + [slot + weights[bit] for slot in held]
+    return stages
+
+
+def expert_kernel(
+    node_count, local_count,
+    hidden_ref, gain_ref, ids_ref, scores_ref, gate_hbm, up_hbm, down_hbm,
+    out_ref,
+    first_rows, second_rows, first_back, second_back, total, tokens, act, gate_w, up_w, down_w,
+    weight_sem, send_sem, recv_sem,
+):
+    width = hidden_ref.shape[1]
+    half, quarter = width // 2, width // 4
+    count = node_count * local_count
+    weights, orders = exchange_orders(node_count, local_count)
+    plans = [gather_plan(weights, order) for order in orders]
+    rows = (first_rows, second_rows)
+    backs = (first_back, second_back)
+    place = {"node": lax.axis_index("node"), "local": lax.axis_index("local")}
+
+    def partner(bit):
+        axis, step = bit
+        return {axis: place[axis] + step - 2 * step * ((place[axis] // step) % 2)}
+
+    loads = [
+        pltpu.make_async_copy(source.at[0], target, weight_sem.at[k])
+        for k, (source, target) in enumerate(
+            ((gate_hbm, gate_w), (up_hbm, up_w), (down_hbm, down_w))
+        )
+    ]
+    for load in loads:
+        load.start()
+    barrier = pltpu.get_barrier_semaphore()
+    for bit in weights:
+        pl.semaphore_signal(
+            barrier, inc=1, device_id=partner(bit), device_id_type=pl.DeviceIdType.MESH
+        )
+
+    hidden = hidden_ref[...].astype(jnp.float32)
+    mean_square = jnp.mean(hidden * hidden, axis=1, keepdims=True)
+    normed = hidden * lax.rsqrt(mean_square + 1e-06) * gain_ref[...].astype(jnp.float32)
+    scores = scores_ref[...]
+    gates = scores / jnp.sum(scores, axis=1, keepdims=True)
+    lanes = lax.broadcasted_iota(jnp.int32, (8, 128), 1)
+    dense = jnp.zeros((8, 128), jnp.float32)
+    for j in range(ids_ref.shape[1]):
+        dense = dense + jnp.where(lanes == ids_ref[:, j : j + 1], gates[:, j : j + 1], 0.0)
+    high = dense.astype(jnp.bfloat16).astype(jnp.float32)
+    for q in range(2):
+        pair = [normed[:, (2 * q + k) * quarter : (2 * q + k + 1) * quarter] for k in range(2)]
+        rows[q][0, :, :quarter] = jnp.concatenate(pair, axis=0).astype(jnp.bfloat16)
+    first_rows[0, :, quarter:] = jnp.concatenate([high, dense - high], axis=0).astype(jnp.bfloat16)
+    pl.semaphore_wait(barrier, len(weights))
+
+    used = 0
+    pending = []
+    for stage in range(len(weights)):
+        arriving = []
+        for q in range(2):
+            bit, runs = plans[q][stage]
+            for start, size in runs:
+                copy = pltpu.make_async_remote_copy(
+                    src_ref=rows[q].at[pl.ds(start, size)],
+                    dst_ref=rows[q].at[pl.ds(start + weights[bit], size)],
+                    send_sem=send_sem.at[used],
+                    recv_sem=recv_sem.at[used],
+                    device_id=partner(bit),
+                    device_id_type=pl.DeviceIdType.MESH,
+                )
+                copy.start()
+                arriving.append(copy)
+                used += 1
+        for copy in arriving:
+            copy.wait_recv()
+        pending += arriving
+    for copy in pending:
+        copy.wait_send()
+    for load in loads:
+        load.wait()
+
+    tile = tokens.shape[0]
+    blocks = tile // 8
+    ff = gate_w.shape[1]
+    mine = (place["node"] * local_count + place["local"]) // 2
+
+    @pl.loop(0, count // blocks)
+    def _(step):
+        at = step * blocks
+        for q in range(2):
+            @pl.loop(0, blocks)
+            def _(b):
+                both = rows[q][at + b, :, :quarter].astype(jnp.float32)
+                into = pl.ds(pl.multiple_of(b * 8, 8), 8)
+                for k in range(2):
+                    columns = slice((2 * q + k) * quarter, (2 * q + k + 1) * quarter)
+                    tokens[into, columns] = both[8 * k : 8 * k + 8]
+        split = first_rows[pl.ds(at, blocks), :, quarter:].astype(jnp.float32)
+        every = (split[:, :8] + split[:, 8:]).reshape(tile, 128)
+        lane = lax.broadcasted_iota(jnp.int32, (tile, 128), 1)
+        gate = jnp.sum(jnp.where(lane == mine, every, 0.0), axis=1, keepdims=True)
+
+        @pl.loop(0, ff // 256)
+        def _(f):
+            columns = pl.ds(pl.multiple_of(f * 256, 256), 256)
+            x = tokens[...].astype(jnp.bfloat16)
+            g = jnp.dot(x, gate_w[:, columns], preferred_element_type=jnp.float32)
+            u = jnp.dot(x, up_w[:, columns], preferred_element_type=jnp.float32)
+            act[:, columns] = (g / (1.0 + jnp.exp(-g)) * u).astype(jnp.bfloat16)
+
+        @pl.loop(0, width // 512)
+        def _(c):
+            columns = pl.ds(pl.multiple_of(c * 512, 512), 512)
+            made = jnp.dot(act[...], down_w[:, columns], preferred_element_type=jnp.float32)
+            total[pl.ds(at, blocks), :, columns] = (made * gate).reshape(blocks, 8, 512)
+
+    pending = []
+    for stage in reversed(range(len(weights))):
+        arriving = []
+        for q in range(2):
+            bit, runs = plans[q][stage]
+            weight = weights[bit]
+            for start, size in runs:
+                @pl.loop(start + weight, start + weight + size)
+                def _(p):
+                    pair = [
+                        total[p, :, (2 * q + k) * quarter : (2 * q + k + 1) * quarter]
+                        for k in range(2)
+                    ]
+                    rows[q][p, :, :quarter] = jnp.concatenate(pair, axis=0).astype(jnp.bfloat16)
+
+                span = pl.ds(start + weight, size)
+                copy = pltpu.make_async_remote_copy(
+                    src_ref=rows[q].at[span, :, pl.ds(0, quarter)],
+                    dst_ref=backs[q].at[span],
+                    send_sem=send_sem.at[used],
+                    recv_sem=recv_sem.at[used],
+                    device_id=partner(bit),
+                    device_id_type=pl.DeviceIdType.MESH,
+                )
+                copy.start()
+                arriving.append((q, start, size, weight, copy))
+                used += 1
+        for q, start, size, weight, copy in arriving:
+            copy.wait_recv()
+
+            @pl.loop(start, start + size)
+            def _(p):
+                both = backs[q][p + weight].astype(jnp.float32)
+                for k in range(2):
+                    columns = slice((2 * q + k) * quarter, (2 * q + k + 1) * quarter)
+                    total[p, :, columns] += both[8 * k : 8 * k + 8]
+            pending.append(copy)
+    out_ref[...] = total[0].astype(out_ref.dtype)
+    for copy in pending:
+        copy.wait_send()
+
+
+def routed_experts(
+    hidden_rows, norm_gain, expert_ids, route_scores, gate_weight, up_weight, down_weight
+):
+    row_count, width = hidden_rows.shape
+    node_count = lax.axis_size("node")
+    local_count = lax.axis_size("local")
+    count = node_count * local_count
+    quarter = width // 4
+    ff = gate_weight.shape[2]
+    weights, orders = exchange_orders(node_count, local_count)
+    copies = sum(len(runs) for order in orders for _, runs in gather_plan(weights, order))
+    tile = min(256, count * row_count)
+    vmem = pl.BlockSpec(memory_space=pltpu.VMEM)
+    anywhere = pl.BlockSpec(memory_space=pl.ANY)
+    rows = count * row_count
+    return pl.pallas_call(
+        functools.partial(expert_kernel, node_count, local_count),
+        out_shape=jax.ShapeDtypeStruct((row_count, width), jnp.bfloat16),
+        in_specs=[vmem] * 4 + [anywhere] * 3,
+        out_specs=vmem,
+        scratch_shapes=[
+            pltpu.VMEM((count, 16, quarter + 128), jnp.bfloat16),
+            pltpu.VMEM((count, 16, quarter), jnp.bfloat16),
+            pltpu.VMEM((count, 16, quarter), jnp.bfloat16),
+            pltpu.VMEM((count, 16, quarter), jnp.bfloat16),
+            pltpu.VMEM((count, 8, width), jnp.float32),
+            pltpu.VMEM((tile, width), jnp.float32),
+            pltpu.VMEM((tile, ff), jnp.bfloat16),
+            pltpu.VMEM((width, ff), jnp.bfloat16),
+            pltpu.VMEM((width, ff), jnp.bfloat16),
+            pltpu.VMEM((ff, width), jnp.bfloat16),
+            pltpu.SemaphoreType.DMA((3,)),
+            pltpu.SemaphoreType.DMA((2 * copies,)),
+            pltpu.SemaphoreType.DMA((2 * copies,)),
+        ],
+        compiler_params=pltpu.CompilerParams(
+            collective_id=0, has_side_effects=True, vmem_limit_bytes=62 * 1024 * 1024
+        ),
+        cost_estimate=pl.CostEstimate(
+            flops=6 * rows * width * ff, bytes_accessed=6 * width * ff, transcendentals=rows * ff
+        ),
+    )(
+        hidden_rows, norm_gain.reshape(1, width), expert_ids, route_scores,
+        gate_weight, up_weight, down_weight,
+    )
 
 
 def per_device(
@@ -65,32 +286,9 @@
     down_weight,
 ):
     context = attend(queries, key_cache, value_cache, fresh_token_keys, new_values, lengths)
-    row_count, model_width = hidden_rows.shape
-    axes = ("node", "local")
-    devices = lax.axis_size("node") * lax.axis_size("local")
-    experts = devices // 2
-    hidden_f32 = hidden_rows.astype(jnp.float32)
-    mean_square = jnp.mean(hidden_f32 * hidden_f32, axis=1, keepdims=True)
-    normed = (hidden_f32 * lax.rsqrt(mean_square + 1e-06) * norm_gain.astype(jnp.float32)).astype(
-        jnp.bfloat16
-    )
-    gates = route_scores / jnp.sum(route_scores, axis=1, keepdims=True)
-    matches = expert_ids[:, :, None] == jnp.arange(experts, dtype=jnp.int32)[None, None, :]
-    dense_gates = jnp.sum(jnp.where(matches, gates[:, :, None], 0.0), axis=1)
-    tokens = lax.all_gather(normed, axes, axis=0, tiled=True)
-    all_gates = lax.all_gather(dense_gates, axes, axis=0, tiled=True)
-    mine = (lax.axis_index("node") * lax.axis_size("local") + lax.axis_index("local")) // 2
-    column = jnp.sum(
-        jnp.where(jnp.arange(experts, dtype=jnp.int32)[None, :] == mine, all_gates, 0.0),
-        axis=1,
-        keepdims=True,
-    )
-    produced = routed_expert_rows(tokens, gate_weight[0], up_weight[0], down_weight[0])
-    weighted = (produced * column).astype(jnp.bfloat16)
-    returned = lax.all_to_all(
-        weighted.reshape(devices, row_count, model_width), axes, split_axis=0, concat_axis=0, tiled=True
-    )
-    weighted_expert_total = jnp.sum(returned.astype(jnp.float32), axis=0).astype(jnp.bfloat16)
+    weighted_expert_total = routed_experts(
+        hidden_rows, norm_gain, expert_ids, route_scores, gate_weight, up_weight, down_weight
+    )
     return (context, weighted_expert_total)
 
 

time: 160 us -> 69 us (0.43)
  blocking collectives: 71 us -> 0 us
  Pallas kernels: 0 us -> 59.4 us
  waiting for transfers between devices: 44 us -> 0 us
  matrix products: 19.4 us -> 3.28 us
  between operations: 14.2 us -> 0.67 us
  other arithmetic: 7.09 us -> 1.84 us
  starting transfers between devices: 2.91 us -> 0 us
  local copies, waits for them, and re-layouts: 0.78 us -> 3.55 us
    all_gather x1 -> x0, blocking collectives: 71 us -> none  [per_device(): all_gates = lax.all_gather(dense_gates, axes, axis=0, tiled=True)]
    pallas_call x0 -> x1, Pallas kernels: none -> 59.4 us  [routed_experts(): pl.pallas_call(functools.partial(expert_kernel, node_count, local_count),...]
    all_to_all x1 -> x0, waiting for transfers between devices: 44 us -> none  [per_device(): lax.all_to_all(weighted.reshape(devices, row_count, model_width), axes, s...]
    dot_general x2 -> x0, matrix products: 17 us -> none  [the longest x1 10.8 us: routed_expert_rows(): return jnp.dot(activated, down_piece, preferred_element_type=jnp.float32)]
    reduce_sum x5 -> x0, other arithmetic: 3.6 us -> none  [the longest x1 0.99 us: per_device(): mean_square = jnp.mean(hidden_f32 * hidden_f32, axis=1, keepdims=True)]
    all_to_all x1 -> x0, starting transfers between devices: 2.87 us -> none  [per_device(): lax.all_to_all(weighted.reshape(devices, row_count, model_width), axes, s...]
    convert_element_type x2 -> x0, other arithmetic: 2.32 us -> none  [the longest x1 1.56 us: per_device(): (hidden_f32 * lax.rsqrt(mean_square + 1e-06) * norm_gain.astype(jnp.float...]
  transfers between devices with their start and end apart: 2 -> 0, of which waited for: 1 -> 0; matrix products, arithmetic and copies ran while one was open for 4% -> 0% of each run, Pallas kernels for 0% -> 0%
where the time goes in v2:
time: 69 us; the launch traced here: 68.7 us
  Pallas kernels  59.4 us (86%)
  local copies, waits for them, and re-layouts  3.55 us (5%)
  matrix products  3.28 us (5%)
  other arithmetic  1.84 us (3%)
    pallas_call x1, Pallas kernels, routed_experts(): pl.pallas_call(functools.partial(expert_kernel, node_count, local_count),...  59.4 us
    unnamed x4, local copies, waits for them, and re-layouts  2.24 us
    dot_general x1, matrix products, attend(): jnp.einsum('bkgd,bkpd->bkgp', grouped_queries, key_cache, preferred_eleme...  1.81 us

profile of v2, /device:TPU:0, one launch (start us, length us, event | category | flops | bytes accessed | tf_op | source)
XLA Modules:
  0.0 68.7 jit_solution(593676129556402196)
XLA Ops:
  0.6 0.0 copy-start
  0.6 0.8 %iota_compare_fusion = pred[8,96]{1,0:T(8,128)(4,1)S(1)} fusion(s32[8]{0:T(128)} %param.18), kind=kLoop, calls=%fused_computation.16 | loop fusion | flops 768 | bytes 800 | tf_op jit(solution)/shard_map/lt | solution.py:25
  1.4 1.8 %fusion.9 = (f32[8,4,16]{2,1,0:T(4,128)S(1)}, f32[8,4,16,96]{3,2,1,0:T(8,128)S(1)}) fusion(bf16[8,4,16,128]{3,2,1,0:T(8,128)(2,1)} %bitcast.15, bf16[8,4,96,128]{3,2,1,0:T(8,128)(2,1)} %param.14, pred[8,96]{1,0:T(8,128)(4,1)S(1)} %iota_compare_fusion), kind=kOutput, calls=%fused_computation.18 | convolution fusion | flops 12729856 | bytes 1116928 | tf_op jit(solution)/shard_map/bkgd,bkpd->bkgp/dot_general | solution.py:19
  3.3 1.1 %fusion.5 = f32[8,4,1,16]{3,2,1,0:T(1,128)S(1)} fusion(bf16[8,4,16,128]{3,2,1,0:T(8,128)(2,1)} %bitcast.16, bf16[8,4,128,1]{2,1,0,3:T(4,128)(2,1)} %bitcast.19), kind=kOutput, calls=%fused_computation.10 | convolution fusion | flops 131072 | bytes 141312 | tf_op jit(solution)/shard_map/uxea,uxa->uxe/dot_general | solution.py:28
  4.4 0.3 fusion.2
  4.7 0.7 %convert_element_type.21 = f32[8,4,128]{2,1,0:T(4,128)S(1)} convert(bf16[8,4,128]{2,1,0:T(4,128)(2,1)} %param.17) | non-fusion elementwise | flops 4096 | bytes 24576 | tf_op jit(solution)/shard_map/convert_element_type | solution.py:42
  5.4 0.0 copy-done
  5.4 0.4 fusion.1
  5.8 0.8 %copy.21 = bf16[1,8,64,128]{3,1,2,0:T(8,128)(2,1)} copy(bf16[1,8,64,128]{3,2,1,0:T(8,128)(2,1)S(1)} %bitcast.14) | data formatting | bytes 262144
  6.5 1.3 %reshape.34.gain_ref = bf16[1,4096]{1,0:T(2,128)(2,1)} reshape(bf16[4096]{0:T(1024)(128)(2,1)} %param.20) | data formatting | bytes 16384 | tf_op jit(solution)/shard_map/reshape | solution.py:268
  7.9 59.4 %shard_map.140 = bf16[8,4096]{1,0:T(8,128)(2,1)} custom-call(bf16[8,4096]{1,0:T(8,128)(2,1)} %hidden_ref.1, bf16[1,4096]{1,0:T(2,128)(2,1)} %reshape.34.gain_ref, s32[8,8]{1,0:T(8,128)} %ids_ref.1, f32[8,8]{1,0:T(8,128)} %scores_ref.1, bf16[1,4096,768]{2,1,0:T(8,128)(2,1)} %gate_hbm.1, bf16[1,4096,768]{2,1,0:T(8,128)(2,1)} %up_hbm.1, ...), custom_call_target="tpu_custom_call" | custom-call | flops 4831838208 | bytes 18874368 | tf_op jit(solution)/shard_map/pallas_call | solution.py:241
  67.2 1.5 %copy.23 = bf16[8,4096]{1,0:T(8,128)(2,1)} copy(bf16[8,4096]{1,0:T(8,128)(2,1)} %shard_map.140) | data formatting | bytes 131072
  (2 shorter events, 0.1 us)
Async XLA Ops:
  0.6 4.8 %copy-start = (bf16[8,4,96,128]{3,2,1,0:T(8,128)(2,1)S(1)}, bf16[8,4,96,128]{3,2,1,0:T(8,128)(2,1)}, u32[]{:S(2)}) copy-start(bf16[8,4,96,128]{3,2,1,0:T(8,128)(2,1)} %param.15) | copy-start | bytes 2359300

commit v3 on v2

--- a/solution.py
+++ b/solution.py
@@ -49,7 +49,9 @@
     node_bits = [("node", 1 << b) for b in reversed(range(1, node_count.bit_length() - 1))]
     core = [("node", 1)]
     weights = {bit: 1 << k for k, bit in enumerate(local_bits + node_bits + core)}
-    return weights, (local_bits + node_bits + core, local_bits + node_bits[::-1] + core)
+    forward = local_bits + node_bits + core
+    backward = local_bits + node_bits[::-1] + core
+    return weights, (forward, backward, forward, backward)
 
 
 def runs_of(slots):
@@ -73,17 +75,16 @@
 def expert_kernel(
     node_count, local_count,
     hidden_ref, gain_ref, ids_ref, scores_ref, gate_hbm, up_hbm, down_hbm,
-    out_ref,
-    first_rows, second_rows, first_back, second_back, total, tokens, act, gate_w, up_w, down_w,
-    weight_sem, send_sem, recv_sem,
+    out_ref, *scratch,
 ):
+    rows, backs = scratch[:4], scratch[4:8]
+    total, tokens, act, gate_rows, gate_w, up_w, down_w = scratch[8:15]
+    weight_sem, send_sem, recv_sem = scratch[15:]
     width = hidden_ref.shape[1]
-    half, quarter = width // 2, width // 4
+    part, piece = width // 4, width // 8
     count = node_count * local_count
     weights, orders = exchange_orders(node_count, local_count)
     plans = [gather_plan(weights, order) for order in orders]
-    rows = (first_rows, second_rows)
-    backs = (first_back, second_back)
     place = {"node": lax.axis_index("node"), "local": lax.axis_index("local")}
 
     def partner(bit):
@@ -106,7 +107,9 @@
 
     hidden = hidden_ref[...].astype(jnp.float32)
     mean_square = jnp.mean(hidden * hidden, axis=1, keepdims=True)
-    normed = hidden * lax.rsqrt(mean_square + 1e-06) * gain_ref[...].astype(jnp.float32)
+    gain = gain_ref[...].astype(jnp.float32)
+    gain = jnp.concatenate([gain[k : k + 1] for k in range(width // 128)], axis=1)
+    normed = hidden * lax.rsqrt(mean_square + 1e-06) * gain
     scores = scores_ref[...]
     gates = scores / jnp.sum(scores, axis=1, keepdims=True)
     lanes = lax.broadcasted_iota(jnp.int32, (8, 128), 1)
@@ -114,17 +117,20 @@
     for j in range(ids_ref.shape[1]):
         dense = dense + jnp.where(lanes == ids_ref[:, j : j + 1], gates[:, j : j + 1], 0.0)
     high = dense.astype(jnp.bfloat16).astype(jnp.float32)
-    for q in range(2):
-        pair = [normed[:, (2 * q + k) * quarter : (2 * q + k + 1) * quarter] for k in range(2)]
-        rows[q][0, :, :quarter] = jnp.concatenate(pair, axis=0).astype(jnp.bfloat16)
-    first_rows[0, :, quarter:] = jnp.concatenate([high, dense - high], axis=0).astype(jnp.bfloat16)
+    for q in range(4):
+        pair = [normed[:, q * part + k * piece : q * part + (k + 1) * piece] for k in range(2)]
+        rows[q][0, :, :piece] = jnp.concatenate(pair, axis=0).astype(jnp.bfloat16)
+    rows[0][0, :, piece:] = jnp.concatenate([high, dense - high], axis=0).astype(jnp.bfloat16)
     pl.semaphore_wait(barrier, len(weights))
 
     used = 0
     pending = []
+    arriving = [[], [], [], []]
     for stage in range(len(weights)):
-        arriving = []
-        for q in range(2):
+        for q in range(4):
+            for copy in arriving[q]:
+                copy.wait_recv()
+            arriving[q] = []
             bit, runs = plans[q][stage]
             for start, size in runs:
                 copy = pltpu.make_async_remote_copy(
@@ -136,88 +142,120 @@
                     device_id_type=pl.DeviceIdType.MESH,
                 )
                 copy.start()
-                arriving.append(copy)
+                arriving[q].append(copy)
+                pending.append(copy)
                 used += 1
-        for copy in arriving:
-            copy.wait_recv()
-        pending += arriving
-    for copy in pending:
-        copy.wait_send()
-    for load in loads:
-        load.wait()
 
     tile = tokens.shape[0]
     blocks = tile // 8
     ff = gate_w.shape[1]
     mine = (place["node"] * local_count + place["local"]) // 2
 
+    def assemble(q, at):
+        @pl.loop(0, blocks // 2)
+        def _(b):
+            one = rows[q][at + 2 * b, :, :piece].astype(jnp.float32)
+            two = rows[q][at + 2 * b + 1, :, :piece].astype(jnp.float32)
+            into = pl.ds(pl.multiple_of(b * 16, 16), 16)
+            for k in range(2):
+                both = jnp.concatenate([one[8 * k : 8 * k + 8], two[8 * k : 8 * k + 8]], axis=0)
+                columns = slice(q * part + k * piece, q * part + (k + 1) * piece)
+                tokens[into, columns] = both.astype(jnp.bfloat16)
+
+    for q in range(4):
+        for copy in arriving[q]:
+            copy.wait_recv()
+        assemble(q, 0)
+    for load in loads:
+        load.wait()
+
     @pl.loop(0, count // blocks)
     def _(step):
         at = step * blocks
-        for q in range(2):
-            @pl.loop(0, blocks)
-            def _(b):
-                both = rows[q][at + b, :, :quarter].astype(jnp.float32)
-                into = pl.ds(pl.multiple_of(b * 8, 8), 8)
-                for k in range(2):
-                    columns = slice((2 * q + k) * quarter, (2 * q + k + 1) * quarter)
-                    tokens[into, columns] = both[8 * k : 8 * k + 8]
-        split = first_rows[pl.ds(at, blocks), :, quarter:].astype(jnp.float32)
+        into = pl.ds(pl.multiple_of(step * tile, tile), tile)
+
+        @pl.when(step > 0)
+        def _():
+            for q in range(4):
+                assemble(q, at)
+
+        split = rows[0][pl.ds(at, blocks), :, piece:].astype(jnp.float32)
         every = (split[:, :8] + split[:, 8:]).reshape(tile, 128)
         lane = lax.broadcasted_iota(jnp.int32, (tile, 128), 1)
         gate = jnp.sum(jnp.where(lane == mine, every, 0.0), axis=1, keepdims=True)
+        gate_rows[into, :] = jnp.broadcast_to(gate, (tile, 128))
 
         @pl.loop(0, ff // 256)
         def _(f):
             columns = pl.ds(pl.multiple_of(f * 256, 256), 256)
-            x = tokens[...].astype(jnp.bfloat16)
-            g = jnp.dot(x, gate_w[:, columns], preferred_element_type=jnp.float32)
-            u = jnp.dot(x, up_w[:, columns], preferred_element_type=jnp.float32)
-            act[:, columns] = (g / (1.0 + jnp.exp(-g)) * u).astype(jnp.bfloat16)
-
-        @pl.loop(0, width // 512)
-        def _(c):
-            columns = pl.ds(pl.multiple_of(c * 512, 512), 512)
-            made = jnp.dot(act[...], down_w[:, columns], preferred_element_type=jnp.float32)
-            total[pl.ds(at, blocks), :, columns] = (made * gate).reshape(blocks, 8, 512)
-
-    pending = []
-    for stage in reversed(range(len(weights))):
-        arriving = []
-        for q in range(2):
-            bit, runs = plans[q][stage]
-            weight = weights[bit]
-            for start, size in runs:
-                @pl.loop(start + weight, start + weight + size)
-                def _(p):
-                    pair = [
-                        total[p, :, (2 * q + k) * quarter : (2 * q + k + 1) * quarter]
-                        for k in range(2)
-                    ]
-                    rows[q][p, :, :quarter] = jnp.concatenate(pair, axis=0).astype(jnp.bfloat16)
-
-                span = pl.ds(start + weight, size)
-                copy = pltpu.make_async_remote_copy(
-                    src_ref=rows[q].at[span, :, pl.ds(0, quarter)],
-                    dst_ref=backs[q].at[span],
-                    send_sem=send_sem.at[used],
-                    recv_sem=recv_sem.at[used],
-                    device_id=partner(bit),
-                    device_id_type=pl.DeviceIdType.MESH,
-                )
-                copy.start()
-                arriving.append((q, start, size, weight, copy))
-                used += 1
-        for q, start, size, weight, copy in arriving:
+            g = jnp.dot(tokens[...], gate_w[:, columns], preferred_element_type=jnp.float32)
+            u = jnp.dot(tokens[...], up_w[:, columns], preferred_element_type=jnp.float32)
+            act[into, columns] = (g / (1.0 + jnp.exp(-g)) * u).astype(jnp.bfloat16)
+
+    for copy in pending:
+        copy.wait_send()
+
+    def send_back(q, stage, used):
+        bit, runs = plans[q][stage]
+        weight = weights[bit]
+        started = []
+        for start, size in runs:
+            @pl.loop(start + weight, start + weight + size)
+            def _(p):
+                pair = [
+                    total[p, :, q * part + k * piece : q * part + (k + 1) * piece]
+                    for k in range(2)
+                ]
+                rows[q][p, :, :piece] = jnp.concatenate(pair, axis=0).astype(jnp.bfloat16)
+
+            span = pl.ds(start + weight, size)
+            copy = pltpu.make_async_remote_copy(
+                src_ref=rows[q].at[span, :, pl.ds(0, piece)],
+                dst_ref=backs[q].at[span],
+                send_sem=send_sem.at[used],
+                recv_sem=recv_sem.at[used],
+                device_id=partner(bit),
+                device_id_type=pl.DeviceIdType.MESH,
+            )
+            copy.start()
+            started.append((start, size, weight, copy))
+            used += 1
+        return started, used
+
+    def take_back(q, started):
+        for start, size, weight, copy in started:
             copy.wait_recv()
 
             @pl.loop(start, start + size)
             def _(p):
                 both = backs[q][p + weight].astype(jnp.float32)
                 for k in range(2):
-                    columns = slice((2 * q + k) * quarter, (2 * q + k + 1) * quarter)
+                    columns = slice(q * part + k * piece, q * part + (k + 1) * piece)
                     total[p, :, columns] += both[8 * k : 8 * k + 8]
-            pending.append(copy)
+
+    pending = []
+    last = len(weights) - 1
+    for stage in reversed(range(len(weights))):
+        for q in range(4):
+            if stage == last:
+                @pl.loop(0, count // blocks)
+                def _(step):
+                    into = pl.ds(pl.multiple_of(step * tile, tile), tile)
+                    for k in range(2):
+                        columns = slice(q * part + k * piece, q * part + (k + 1) * piece)
+                        made = jnp.dot(
+                            act[into, :], down_w[:, columns], preferred_element_type=jnp.float32
+                        )
+                        made = made * gate_rows[into, :1]
+                        total[pl.ds(step * blocks, blocks), :, columns] = made.reshape(
+                            blocks, 8, piece
+                        )
+            else:
+                take_back(q, arriving[q])
+            arriving[q], used = send_back(q, stage, used)
+            pending += [entry[3] for entry in arriving[q]]
+    for q in range(4):
+        take_back(q, arriving[q])
     out_ref[...] = total[0].astype(out_ref.dtype)
     for copy in pending:
         copy.wait_send()
@@ -230,7 +268,7 @@
     node_count = lax.axis_size("node")
     local_count = lax.axis_size("local")
     count = node_count * local_count
-    quarter = width // 4
+    piece = width // 8
     ff = gate_weight.shape[2]
     weights, orders = exchange_orders(node_count, local_count)
     copies = sum(len(runs) for order in orders for _, runs in gather_plan(weights, order))
@@ -244,13 +282,12 @@
         in_specs=[vmem] * 4 + [anywhere] * 3,
         out_specs=vmem,
         scratch_shapes=[
-            pltpu.VMEM((count, 16, quarter + 128), jnp.bfloat16),
-            pltpu.VMEM((count, 16, quarter), jnp.bfloat16),
-            pltpu.VMEM((count, 16, quarter), jnp.bfloat16),
-            pltpu.VMEM((count, 16, quarter), jnp.bfloat16),
+            pltpu.VMEM((count, 16, piece + 128), jnp.bfloat16),
+            *[pltpu.VMEM((count, 16, piece), jnp.bfloat16)] * 7,
             pltpu.VMEM((count, 8, width), jnp.float32),
-            pltpu.VMEM((tile, width), jnp.float32),
-            pltpu.VMEM((tile, ff), jnp.bfloat16),
+            pltpu.VMEM((tile, width), jnp.bfloat16),
+            pltpu.VMEM((rows, ff), jnp.bfloat16),
+            pltpu.VMEM((rows, 128), jnp.float32),
             pltpu.VMEM((width, ff), jnp.bfloat16),
             pltpu.VMEM((width, ff), jnp.bfloat16),
             pltpu.VMEM((ff, width), jnp.bfloat16),
@@ -265,7 +302,7 @@
             flops=6 * rows * width * ff, bytes_accessed=6 * width * ff, transcendentals=rows * ff
         ),
     )(
-        hidden_rows, norm_gain.reshape(1, width), expert_ids, route_scores,
+        hidden_rows, norm_gain.reshape(width // 128, 128), expert_ids, route_scores,
         gate_weight, up_weight, down_weight,
     )
 

time: 69 us -> 59.3 us (0.86)
  Pallas kernels: 59.4 us -> 51 us
  local copies, waits for them, and re-layouts: 3.55 us -> 2.24 us
    pallas_call x1, Pallas kernels: 59.4 us -> 51 us  [routed_experts(): pl.pallas_call(functools.partial(expert_kernel, node_count, local_count),...]
    reshape x1 -> x0, local copies, waits for them, and re-layouts: 1.31 us -> none  [routed_experts(): norm_gain.reshape(1, width)]
where the time goes in v3:
time: 59.3 us; the launch traced here: 59 us
  Pallas kernels  51 us (86%)
  matrix products  3.28 us (6%)
  local copies, waits for them, and re-layouts  2.24 us (4%)
  other arithmetic  1.84 us (3%)
  between operations  0.67 us (1%)
    pallas_call x1, Pallas kernels, routed_experts(): pl.pallas_call(functools.partial(expert_kernel, node_count, local_count),...  51 us
    unnamed x4, local copies, waits for them, and re-layouts  2.24 us
    dot_general x1, matrix products, attend(): jnp.einsum('bkgd,bkpd->bkgp', grouped_queries, key_cache, preferred_eleme...  1.81 us

profile of v3, /device:TPU:0, one launch (start us, length us, event | category | flops | bytes accessed | tf_op | source)
XLA Modules:
  0.0 59.0 jit_solution(5853033986924972449)
XLA Ops:
  0.6 0.0 copy-start
  0.6 0.8 %iota_compare_fusion = pred[8,96]{1,0:T(8,128)(4,1)S(1)} fusion(s32[8]{0:T(128)} %param.18), kind=kLoop, calls=%fused_computation.16 | loop fusion | flops 768 | bytes 800 | tf_op jit(solution)/shard_map/lt | solution.py:25
  1.4 1.8 %fusion.9 = (f32[8,4,16]{2,1,0:T(4,128)S(1)}, f32[8,4,16,96]{3,2,1,0:T(8,128)S(1)}) fusion(bf16[8,4,16,128]{3,2,1,0:T(8,128)(2,1)} %bitcast.16, bf16[8,4,96,128]{3,2,1,0:T(8,128)(2,1)} %param.14, pred[8,96]{1,0:T(8,128)(4,1)S(1)} %iota_compare_fusion), kind=kOutput, calls=%fused_computation.18 | convolution fusion | flops 12729856 | bytes 1116928 | tf_op jit(solution)/shard_map/bkgd,bkpd->bkgp/dot_general | solution.py:19
  3.3 1.1 %fusion.5 = f32[8,4,1,16]{3,2,1,0:T(1,128)S(1)} fusion(bf16[8,4,16,128]{3,2,1,0:T(8,128)(2,1)} %bitcast.17, bf16[8,4,128,1]{2,1,0,3:T(4,128)(2,1)} %bitcast.21), kind=kOutput, calls=%fused_computation.10 | convolution fusion | flops 131072 | bytes 141312 | tf_op jit(solution)/shard_map/uxea,uxa->uxe/dot_general | solution.py:28
  4.4 0.3 fusion.2
  4.7 0.7 %convert_element_type.21 = f32[8,4,128]{2,1,0:T(4,128)S(1)} convert(bf16[8,4,128]{2,1,0:T(4,128)(2,1)} %param.17) | non-fusion elementwise | flops 4096 | bytes 24576 | tf_op jit(solution)/shard_map/convert_element_type | solution.py:42
  5.4 0.0 copy-done
  5.4 0.4 fusion.1
  5.8 0.8 %copy.21 = bf16[1,8,64,128]{3,1,2,0:T(8,128)(2,1)} copy(bf16[1,8,64,128]{3,2,1,0:T(8,128)(2,1)S(1)} %bitcast.15) | data formatting | bytes 262144
  6.5 51.0 %shard_map.140 = bf16[8,4096]{1,0:T(8,128)(2,1)} custom-call(bf16[8,4096]{1,0:T(8,128)(2,1)} %hidden_ref.1, bf16[32,128]{1,0:T(8,128)(2,1)} %bitcast.20, s32[8,8]{1,0:T(8,128)} %ids_ref.1, f32[8,8]{1,0:T(8,128)} %scores_ref.1, bf16[1,4096,768]{2,1,0:T(8,128)(2,1)} %gate_hbm.1, bf16[1,4096,768]{2,1,0:T(8,128)(2,1)} %up_hbm.1, bf16[1,768,4096]{2,1,0:T(8,128)(2,1)} %down_hbm.1), custom_call_target="tpu_custom_call" | custom-call | flops 4831838208 | bytes 18874368 | tf_op jit(solution)/shard_map/pallas_call | solution.py:279
  57.5 1.5 %copy.23 = bf16[8,4096]{1,0:T(8,128)(2,1)} copy(bf16[8,4096]{1,0:T(8,128)(2,1)} %shard_map.140) | data formatting | bytes 131072
  (2 shorter events, 0.1 us)
Async XLA Ops:
  0.6 4.8 %copy-start = (bf16[8,4,96,128]{3,2,1,0:T(8,128)(2,1)S(1)}, bf16[8,4,96,128]{3,2,1,0:T(8,128)(2,1)}, u32[]{:S(2)}) copy-start(bf16[8,4,96,128]{3,2,1,0:T(8,128)(2,1)} %param.15) | copy-start | bytes 2359300

commit v4 on v3

--- a/solution.py
+++ b/solution.py
@@ -9,39 +9,30 @@
 from jax.sharding import PartitionSpec as P
 
 
-def attend(queries, key_cache, value_cache, fresh_token_keys, new_values, lengths):
-    request_count, head_count, head_width = queries.shape
-    kv_heads = key_cache.shape[1]
-    slot_count = key_cache.shape[2]
-    grouped_queries = queries.reshape(request_count, kv_heads, head_count // kv_heads, head_width)
+def attend_request(b, queries, keys, values, fresh_keys, new_values, lengths, context):
+    kv_heads, slot_count, head_width = keys.shape[1:]
+    group = queries.shape[1] // kv_heads
     inverse_scale = 1.0 / math.sqrt(head_width)
-    scores = (
-        jnp.einsum(
-            "bkgd,bkpd->bkgp", grouped_queries, key_cache, preferred_element_type=jnp.float32
+    in_range = lax.broadcasted_iota(jnp.int32, (group, slot_count), 1) < lengths[b]
+    fresh = fresh_keys[b].astype(jnp.float32)
+    newest = new_values[b].astype(jnp.float32)
+    for k in range(kv_heads):
+        query = queries[b, k * group : (k + 1) * group]
+        scores = lax.dot_general(
+            query, keys[b, k], (((1,), (1,)), ((), ())), preferred_element_type=jnp.float32
         )
-        * inverse_scale
-    )
-    positions = jnp.arange(slot_count, dtype=jnp.int32)
-    in_range = positions[None, :] < lengths[:, None]
-    scores = jnp.where(in_range[:, None, None, :], scores, -jnp.inf)
-    self_token_score = (
-        jnp.einsum(
-            "uxea,uxa->uxe", grouped_queries, fresh_token_keys, preferred_element_type=jnp.float32
-        )
-        * inverse_scale
-    )
-    highest = jnp.maximum(jnp.max(scores, axis=-1), self_token_score)
-    exponent = jnp.exp(scores - highest[..., None])
-    own_exponent = jnp.exp(self_token_score - highest)
-    denominator = jnp.sum(exponent, axis=-1) + own_exponent
-    probs = (exponent / denominator[..., None]).astype(jnp.bfloat16)
-    own_prob = (own_exponent / denominator).astype(jnp.bfloat16)
-    mixed = jnp.einsum("bkgp,bkpd->bkgd", probs, value_cache, preferred_element_type=jnp.float32)
-    mixed = (
-        mixed
-        + own_prob.astype(jnp.float32)[..., None] * new_values.astype(jnp.float32)[:, :, None, :]
-    )
-    return mixed.reshape(request_count, head_count * head_width).astype(jnp.bfloat16)
+        scores = jnp.where(in_range, scores * inverse_scale, -jnp.inf)
+        own = jnp.sum(query.astype(jnp.float32) * fresh[k : k + 1], axis=1, keepdims=True)
+        own = own * inverse_scale
+        highest = jnp.maximum(jnp.max(scores, axis=1, keepdims=True), own)
+        exponent = jnp.exp(scores - highest)
+        own_exponent = jnp.exp(own - highest)
+        denominator = jnp.sum(exponent, axis=1, keepdims=True) + own_exponent
+        probs = (exponent / denominator).astype(jnp.bfloat16)
+        own_prob = (own_exponent / denominator).astype(jnp.bfloat16).astype(jnp.float32)
+        mixed = jnp.dot(probs, values[b, k], preferred_element_type=jnp.float32)
+        mixed = mixed + own_prob * newest[k : k + 1]
+        context[b, k * group : (k + 1) * group] = mixed.astype(jnp.bfloat16)
 
 
 def exchange_orders(node_count, local_count):
@@ -74,12 +65,13 @@
 
 def expert_kernel(
     node_count, local_count,
-    hidden_ref, gain_ref, ids_ref, scores_ref, gate_hbm, up_hbm, down_hbm,
-    out_ref, *scratch,
+    queries, fresh_keys, new_values, lengths, hidden_ref, gain_ref, ids_ref, scores_ref,
+    key_hbm, value_hbm, gate_hbm, up_hbm, down_hbm,
+    context, out_ref, *scratch,
 ):
     rows, backs = scratch[:4], scratch[4:8]
     total, tokens, act, gate_rows, gate_w, up_w, down_w = scratch[8:15]
-    weight_sem, send_sem, recv_sem = scratch[15:]
+    keys, values, weight_sem, send_sem, recv_sem = scratch[15:]
     width = hidden_ref.shape[1]
     part, piece = width // 4, width // 8
     count = node_count * local_count
@@ -97,7 +89,11 @@
             ((gate_hbm, gate_w), (up_hbm, up_w), (down_hbm, down_w))
         )
     ]
-    for load in loads:
+    caches = [
+        pltpu.make_async_copy(key_hbm, keys, weight_sem.at[3]),
+        pltpu.make_async_copy(value_hbm, values, weight_sem.at[4]),
+    ]
+    for load in caches + loads:
         load.start()
     barrier = pltpu.get_barrier_semaphore()
     for bit in weights:
@@ -145,6 +141,17 @@
                 arriving[q].append(copy)
                 pending.append(copy)
                 used += 1
+        turn = stage - max(0, len(weights) - 3)
+        if turn == 0:
+            for load in caches:
+                load.wait()
+        if turn >= 0:
+            requests = queries.shape[0]
+            @pl.loop(turn * requests // 3, (turn + 1) * requests // 3)
+            def _(b):
+                attend_request(
+                    b, queries, keys, values, fresh_keys, new_values, lengths, context
+                )
 
     tile = tokens.shape[0]
     blocks = tile // 8
@@ -261,8 +268,8 @@
         copy.wait_send()
 
 
-def routed_experts(
-    hidden_rows, norm_gain, expert_ids, route_scores, gate_weight, up_weight, down_weight
+def attention_and_experts(
+    queries, key_cache, value_cache, fresh_token_keys, new_values, lengths, hidden_rows, norm_gain, expert_ids, route_scores, gate_weight, up_weight, down_weight
 ):
     row_count, width = hidden_rows.shape
     node_count = lax.axis_size("node")
@@ -278,9 +285,15 @@
     rows = count * row_count
     return pl.pallas_call(
         functools.partial(expert_kernel, node_count, local_count),
-        out_shape=jax.ShapeDtypeStruct((row_count, width), jnp.bfloat16),
-        in_specs=[vmem] * 4 + [anywhere] * 3,
-        out_specs=vmem,
+        out_shape=(
+            jax.ShapeDtypeStruct(queries.shape, jnp.bfloat16),
+            jax.ShapeDtypeStruct((row_count, width), jnp.bfloat16),
+        ),
+        in_specs=[vmem] * 3
+        + [pl.BlockSpec(memory_space=pltpu.SMEM)]
+        + [vmem] * 4
+        + [anywhere] * 5,
+        out_specs=(vmem, vmem),
         scratch_shapes=[
             pltpu.VMEM((count, 16, piece + 128), jnp.bfloat16),
             *[pltpu.VMEM((count, 16, piece), jnp.bfloat16)] * 7,
@@ -291,7 +304,9 @@
             pltpu.VMEM((width, ff), jnp.bfloat16),
             pltpu.VMEM((width, ff), jnp.bfloat16),
             pltpu.VMEM((ff, width), jnp.bfloat16),
-            pltpu.SemaphoreType.DMA((3,)),
+            pltpu.VMEM(key_cache.shape, jnp.bfloat16),
+            pltpu.VMEM(value_cache.shape, jnp.bfloat16),
+            pltpu.SemaphoreType.DMA((5,)),
             pltpu.SemaphoreType.DMA((2 * copies,)),
             pltpu.SemaphoreType.DMA((2 * copies,)),
         ],
@@ -302,7 +317,9 @@
             flops=6 * rows * width * ff, bytes_accessed=6 * width * ff, transcendentals=rows * ff
         ),
     )(
+        queries, fresh_token_keys, new_values, lengths,
         hidden_rows, norm_gain.reshape(width // 128, 128), expert_ids, route_scores,
+        key_cache, value_cache,
         gate_weight, up_weight, down_weight,
     )
 
@@ -322,10 +339,11 @@
     up_weight,
     down_weight,
 ):
-    context = attend(queries, key_cache, value_cache, fresh_token_keys, new_values, lengths)
-    weighted_expert_total = routed_experts(
-        hidden_rows, norm_gain, expert_ids, route_scores, gate_weight, up_weight, down_weight
+    context, weighted_expert_total = attention_and_experts(
+        queries, key_cache, value_cache, fresh_token_keys, new_values, lengths,
+        hidden_rows, norm_gain, expert_ids, route_scores, gate_weight, up_weight, down_weight,
     )
+    context = context.reshape(queries.shape[0], queries.shape[1] * queries.shape[2])
     return (context, weighted_expert_total)
 
 

time: 59.3 us -> 58.2 us (0.981)
  matrix products: 3.28 us -> 0 us
  Pallas kernels: 51 us -> 54.2 us
  other arithmetic: 1.84 us -> 0 us
  local copies, waits for them, and re-layouts: 2.24 us -> 3.12 us
    dot_general x3 -> x0, matrix products: 3.28 us -> none  [the longest x1 1.81 us: attend(): jnp.einsum('bkgd,bkpd->bkgp', grouped_queries, key_cache, preferred_eleme...]
    pallas_call x1, Pallas kernels: 51 us -> 54.2 us  [attention_and_experts(): pl.pallas_call(functools.partial(expert_kernel, node_count, local_count),...]
    unnamed x4 -> x2, local copies, waits for them, and re-layouts: 2.24 us -> 3.12 us
    lt x1 -> x0, other arithmetic: 0.8 us -> none  [attend(): in_range = positions[None, :] < lengths[:, None]]
    convert_element_type x1 -> x0, other arithmetic: 0.7 us -> none  [attend(): new_values.astype(jnp.float32)[:, :, None, :]]
where the time goes in v4:
time: 58.2 us; the launch traced here: 58 us
  Pallas kernels  54.2 us (93%)
  local copies, waits for them, and re-layouts  3.12 us (5%)
  between operations  0.64 us (1%)
    pallas_call x1, Pallas kernels, attention_and_experts(): pl.pallas_call(functools.partial(expert_kernel, node_count, local_count),...  54.2 us
    unnamed x2, local copies, waits for them, and re-layouts  3.12 us

profile of v4, /device:TPU:0, one launch (start us, length us, event | category | flops | bytes accessed | tf_op | source)
XLA Modules:
  0.0 58.0 jit_solution(10816753564302430202)
XLA Ops:
  0.6 54.2 %shard_map.140 = (bf16[8,64,128]{2,1,0:T(8,128)(2,1)}, bf16[8,4096]{1,0:T(8,128)(2,1)}) custom-call(bf16[8,64,128]{2,1,0:T(8,128)(2,1)} %queries.1, bf16[8,4,128]{2,1,0:T(4,128)(2,1)} %fresh_keys.1, bf16[8,4,128]{2,1,0:T(4,128)(2,1)} %new_values.1, s32[8]{0:T(128)} %lengths.1, bf16[8,4096]{1,0:T(8,128)(2,1)} %hidden_ref.1, bf16[32,128]{1,0:T(8,128)(2,1)} %bitcast.7, ...), custom_call_target="tpu_custom_call" | custom-call | flops 4831838208 | bytes 18874368 | tf_op jit(solution)/shard_map/pallas_call | solution.py:286
  54.9 1.6 %copy.17 = bf16[1,8,64,128]{3,1,2,0:T(8,128)(2,1)} copy(bf16[1,8,64,128]{3,2,1,0:T(8,128)(2,1)} %bitcast.6) | data formatting | bytes 262144
  56.5 1.5 %copy.19 = bf16[8,4096]{1,0:T(8,128)(2,1)} copy(bf16[8,4096]{1,0:T(8,128)(2,1)} %get-tuple-element.9) | data formatting | bytes 131072

commit v5 on v4

--- a/solution.py
+++ b/solution.py
@@ -147,7 +147,7 @@
                 load.wait()
         if turn >= 0:
             requests = queries.shape[0]
-            @pl.loop(turn * requests // 3, (turn + 1) * requests // 3)
+            @pl.loop(turn * requests // 3, (turn + 1) * requests // 3, unroll=True)
             def _(b):
                 attend_request(
                     b, queries, keys, values, fresh_keys, new_values, lengths, context
@@ -207,7 +207,7 @@
         weight = weights[bit]
         started = []
         for start, size in runs:
-            @pl.loop(start + weight, start + weight + size)
+            @pl.loop(start + weight, start + weight + size, unroll=size <= 4)
             def _(p):
                 pair = [
                     total[p, :, q * part + k * piece : q * part + (k + 1) * piece]
@@ -233,7 +233,7 @@
         for start, size, weight, copy in started:
             copy.wait_recv()
 
-            @pl.loop(start, start + size)
+            @pl.loop(start, start + size, unroll=size <= 4)
             def _(p):
                 both = backs[q][p + weight].astype(jnp.float32)
                 for k in range(2):

time: 58.2 us -> 57.8 us (level)
  no operation moved by 1% of the time
where the time goes in v5:
time: 57.8 us; the launch traced here: 57.6 us
  Pallas kernels  53.8 us (93%)
  local copies, waits for them, and re-layouts  3.12 us (5%)
  between operations  0.64 us (1%)
    pallas_call x1, Pallas kernels, attention_and_experts(): pl.pallas_call(functools.partial(expert_kernel, node_count, local_count),...  53.8 us
    unnamed x2, local copies, waits for them, and re-layouts  3.12 us

profile of v5, /device:TPU:0, one launch (start us, length us, event | category | flops | bytes accessed | tf_op | source)
XLA Modules:
  0.0 57.6 jit_solution(4880219695058140695)
XLA Ops:
  0.6 53.8 %shard_map.140 = (bf16[8,64,128]{2,1,0:T(8,128)(2,1)}, bf16[8,4096]{1,0:T(8,128)(2,1)}) custom-call(bf16[8,64,128]{2,1,0:T(8,128)(2,1)} %queries.1, bf16[8,4,128]{2,1,0:T(4,128)(2,1)} %fresh_keys.1, bf16[8,4,128]{2,1,0:T(4,128)(2,1)} %new_values.1, s32[8]{0:T(128)} %lengths.1, bf16[8,4096]{1,0:T(8,128)(2,1)} %hidden_ref.1, bf16[32,128]{1,0:T(8,128)(2,1)} %bitcast.7, ...), custom_call_target="tpu_custom_call" | custom-call | flops 4831838208 | bytes 18874368 | tf_op jit(solution)/shard_map/pallas_call | solution.py:286
  54.5 1.6 %copy.17 = bf16[1,8,64,128]{3,1,2,0:T(8,128)(2,1)} copy(bf16[1,8,64,128]{3,2,1,0:T(8,128)(2,1)} %bitcast.6) | data formatting | bytes 262144
  56.1 1.5 %copy.19 = bf16[8,4096]{1,0:T(8,128)(2,1)} copy(bf16[8,4096]{1,0:T(8,128)(2,1)} %get-tuple-element.9) | data formatting | bytes 131072
